TPU v7x, 128 devices: a whole 4x4x4 slice. The times are simulated.
128 devices in a mesh: group: 4 (over z_lo, core), dp: 32 (over z_hi, y, x).
Axes of the slice: x: 4, y: 4, z: 4 (z_hi: 2, z_lo: 2; z = z_hi * 2 + z_lo), core: 2. Of those that a mesh axis runs over, the one named last changes fastest.
Arguments:
- teacher_feat: bfloat16 [256, 257, 4096], P(('dp', 'group')), may hold values from -6 to 6
- teacher_bottleneck: bfloat16 [4096, 256], replicated, may hold values from -0.09375 to 0.09375
- teacher_proto: bfloat16 [256, 65536], P(None, 'dp')
- student_feat: bfloat16 [4, 256, 257, 1024], P('group', 'dp'), may hold values from -6 to 6
- student_bottleneck: bfloat16 [4, 1024, 256], P('group'), may hold values from -0.1875 to 0.1875
- student_proto: bfloat16 [4, 256, 65536], P('group', None, 'dp')
- mask_index: int32 [256, 16], P('dp'), may hold values from 1 to 256, as said below
- mask_count: int32 [256], replicated, may hold values from 1 to 16, as said below
Outputs:
- grad_proto: float32 [4, 256, 65536], P('group', None, 'dp')
- grad_bottleneck: float32 [4, 1024, 256], P('group', 'dp')
- grad_rows: bfloat16 [4, 256, 17, 1024], P('group', 'dp')
Inputs may be any that keep to these rules, and one draw needn't show every extreme that they name: `mask_index`: the mask slots of one image name distinct patches. `mask_count`: some image has all 16 slots live.
All inputs are finite; a program needn't handle non-finite values.
Results may differ from a plain program's by a relative error of at most 0.039.
Values may be sent and summed in bfloat16 or wider, within the bound.
No kernel may reach another device: no remote copies, remote signals or barrier semaphores. Data moves between devices by JAX's collectives and lax.ppermute only.
A program may use at most 128 MiB of HBM per device.

v0:
```python
import functools

import jax
import jax.numpy as jnp
from jax import lax
from jax.experimental import pallas as pl
from jax.experimental.pallas import tpu as pltpu
from jax.sharding import PartitionSpec as P

teacher_temp = 0.05
student_temp = 0.1
norm_eps = 1e-06
log2e = 1.4426950408889634
never = 1e30
bf16 = jnp.bfloat16
f32 = jnp.float32


def normalize_rows(projected):
    lengths = jnp.sqrt(jnp.sum(projected * projected, axis=-1, keepdims=True) + norm_eps)
    return (projected / lengths, lengths)


def column_of(row):
    wide = jnp.broadcast_to(row, (128, row.shape[1]))
    return jnp.transpose(wide)[:, :1]


def row_of(column):
    wide = jnp.broadcast_to(column, (column.shape[0], 128))
    return jnp.transpose(wide)[:1, :]


def vmem(megabytes):
    return pltpu.CompilerParams(vmem_limit_bytes=megabytes * 2**20)


def row_block(block, width):
    return pl.BlockSpec((block, width), lambda i: (i, 0))


def lane_block(block):
    return pl.BlockSpec((1, 1, block), lambda i: (i, 0, 0))


def whole(array):
    return pl.BlockSpec(array.shape, lambda i: (0,) * array.ndim)


def times_transposed(left, right):
    return lax.dot_general(left, right, (((1,), (1,)), ((), ())), preferred_element_type=f32)


def powers_of(scale, rows_ref, proto_ref, peak_ref, lse_ref, powers_ref):
    logits = jnp.dot(rows_ref[...], proto_ref[...], preferred_element_type=f32)
    peak = jnp.max(logits, axis=-1, keepdims=True) * scale
    powers = jnp.exp2(logits * scale - peak)
    powers_ref[...] = powers.astype(bf16)
    total = jnp.sum(powers, axis=-1, keepdims=True)
    peak_ref[0] = row_of(peak)
    lse_ref[0] = row_of(peak + jnp.log2(total))


def powers_terms_kernel(scale, rows_ref, proto_ref, peak_ref, lse_ref, powers_ref, terms_ref):
    powers_of(scale, rows_ref, proto_ref, peak_ref, lse_ref, powers_ref)
    terms_ref[...] = times_transposed(powers_ref[...], proto_ref[...]).astype(bf16)


def stored_powers(rows, proto, temp, block, fused):
    count, width = rows.shape
    columns = proto.shape[1]
    steps = count // block
    lanes = jax.ShapeDtypeStruct((steps, 1, block), f32)
    specs = [lane_block(block), lane_block(block), row_block(block, columns), row_block(block, width)]
    shapes = [lanes, lanes, jax.ShapeDtypeStruct((count, columns), bf16), jax.ShapeDtypeStruct((count, width), bf16)]
    peak, lse, *stored = pl.pallas_call(
        functools.partial(powers_terms_kernel if fused else powers_of, log2e / temp),
        grid=(steps,),
        in_specs=[row_block(block, width), whole(proto)],
        out_specs=specs if fused else specs[:3],
        out_shape=shapes if fused else shapes[:3],
        compiler_params=vmem(48),
        cost_estimate=pl.CostEstimate(
            flops=2 * (1 + fused) * count * proto.size, bytes_accessed=2 * count * columns, transcendentals=count * columns
        ),
    )(rows, proto)
    return peak.reshape(count), lse.reshape(count), *stored


def terms_kernel(powers_ref, proto_ref, terms_ref):
    terms_ref[...] = times_transposed(powers_ref[...], proto_ref[...]).astype(bf16)


def row_terms(powers, proto, block):
    count, columns = powers.shape
    width = proto.shape[0]
    return pl.pallas_call(
        terms_kernel,
        grid=(count // block,),
        in_specs=[row_block(block, columns), whole(proto)],
        out_specs=row_block(block, width),
        out_shape=jax.ShapeDtypeStruct((count, width), bf16),
        compiler_params=vmem(48),
        cost_estimate=pl.CostEstimate(flops=2 * count * proto.size, bytes_accessed=2 * count * columns, transcendentals=0),
    )(powers, proto)


def combine_kernel(scale_s_ref, scale_t_ref, terms_s_ref, terms_t_ref, out_ref):
    student = column_of(scale_s_ref[0]) * terms_s_ref[...].astype(f32)
    teacher = column_of(scale_t_ref[0]) * terms_t_ref[...].astype(f32)
    out_ref[...] = (student - teacher).astype(bf16)


def combined_terms(scale_s, scale_t, terms_s, terms_t, block):
    count, width = terms_s.shape
    steps = count // block
    return pl.pallas_call(
        combine_kernel,
        grid=(steps,),
        in_specs=[lane_block(block), lane_block(block), row_block(block, width), row_block(block, width)],
        out_specs=row_block(block, width),
        out_shape=jax.ShapeDtypeStruct((count, width), bf16),
        compiler_params=vmem(24),
        cost_estimate=pl.CostEstimate(flops=3 * count * width, bytes_accessed=6 * count * width, transcendentals=0),
    )(scale_s.reshape(steps, 1, block), scale_t.reshape(steps, 1, block), terms_s, terms_t)


def grads_kernel(tile, student_ref, scale_s_ref, scale_t_ref, powers_s_ref, powers_t_ref, grad_ref):
    @pl.when(pl.program_id(0) == 0)
    def _():
        grad_ref[...] = jnp.zeros_like(grad_ref)

    student_T = jnp.transpose(student_ref[...])
    scale_s, scale_t = column_of(scale_s_ref[0]), column_of(scale_t_ref[0])
    for start in range(0, grad_ref.shape[1], tile):
        cols = slice(start, start + tile)
        grad = scale_s * powers_s_ref[:, cols].astype(f32) - scale_t * powers_t_ref[:, cols].astype(f32)
        grad_ref[:, cols] += jnp.dot(student_T, grad.astype(bf16), preferred_element_type=f32)


def proto_gradient(student, scale_s, scale_t, powers_s, powers_t, block, tile=512):
    count, width = student.shape
    columns = powers_s.shape[1]
    steps = count // block
    return pl.pallas_call(
        functools.partial(grads_kernel, tile),
        grid=(steps,),
        in_specs=[row_block(block, width), lane_block(block), lane_block(block), row_block(block, columns), row_block(block, columns)],
        out_specs=pl.BlockSpec((width, columns), lambda i: (0, 0)),
        out_shape=jax.ShapeDtypeStruct((width, columns), f32),
        compiler_params=vmem(48),
        cost_estimate=pl.CostEstimate(
            flops=2 * count * width * columns, bytes_accessed=4 * count * columns, transcendentals=0
        ),
    )(student, scale_s.reshape(steps, 1, block), scale_t.reshape(steps, 1, block), powers_s, powers_t)


def to_all(block, parts):
    return lax.all_to_all(jnp.broadcast_to(block[None], (parts,) + block.shape), "dp", 0, 0)


def slots_of(counts, capacity):
    lengths = counts + 1
    ends = jnp.cumsum(lengths, axis=-1)
    starts = ends - lengths
    slot = jnp.arange(capacity)[None, :, None]
    inside = (slot >= starts[:, None, :]) & (slot < ends[:, None, :])
    live = jnp.any(inside, axis=-1)
    image = jnp.sum(jnp.where(inside, jnp.arange(counts.shape[1]), 0), axis=-1)
    place = jnp.sum(jnp.where(inside, slot - starts[:, None, :], 0), axis=-1)
    share = jnp.sum(jnp.where(inside, 1.0 / counts.astype(f32)[:, None, :], 0.0), axis=-1)
    return image, place, jnp.where(place == 0, 1.0, share), live


def packed_step(
    teacher_feat,
    teacher_bottleneck,
    teacher_proto,
    student_feat,
    student_bottleneck,
    student_proto,
    mask_index,
    mask_count,
    *,
    parts,
    group,
    capacity,
):
    images, masked = mask_index.shape
    slot_count = masked + 1
    width = student_bottleneck.shape[-1]
    teacher_images = teacher_feat.shape[0]
    teacher_count = teacher_images * slot_count
    padded_count = -(-teacher_count // 16) * 16
    block = 8 * capacity if capacity < 110 else 4 * capacity if capacity < 120 else 256
    me = lax.axis_index("dp")
    indices = jnp.concatenate([jnp.zeros((images, 1), jnp.int32), mask_index], axis=1)

    image, place, weight, live = slots_of(mask_count.reshape(parts, images), capacity)
    log_weight = jnp.where(live, jnp.log2(weight / student_temp), -never).reshape(-1)
    mine = lambda array: lax.dynamic_index_in_dim(array, me, 0, keepdims=False)
    my_image, my_place, my_live = mine(image), mine(place), mine(live)
    spread = ((my_image * slot_count + my_place)[:, None] == jnp.arange(images * slot_count)) & my_live[:, None]
    my_rows = jnp.sum(jnp.where(spread, indices.reshape(1, -1), 0), axis=-1)
    spread = spread.astype(bf16)

    student_rows = student_feat[my_image, my_rows]
    student_float, lengths = normalize_rows(jnp.dot(student_rows, student_bottleneck, preferred_element_type=f32))
    student_unit = student_float.astype(bf16)
    every_student = to_all(student_unit, parts).reshape(-1, width)

    first_image = lax.axis_index("group") * teacher_images
    teacher_index = lax.dynamic_slice_in_dim(indices, first_image, teacher_images, 0)
    teacher_rows = teacher_feat[jnp.arange(teacher_images)[:, None], teacher_index].reshape(-1, teacher_feat.shape[-1])
    teacher_unit = normalize_rows(jnp.dot(teacher_rows, teacher_bottleneck, preferred_element_type=f32))[0].astype(bf16)
    teacher_unit = jnp.pad(teacher_unit, ((0, padded_count - teacher_count), (0, 0)))
    others = [lax.ppermute(teacher_unit, "group", [(i, i ^ k) for i in range(group)]) for k in range(1, group)]
    group_teacher = jnp.concatenate([teacher_unit] + others)
    owner = (my_image // teacher_images) ^ lax.axis_index("group")
    held = owner * padded_count + (my_image % teacher_images) * slot_count + my_place
    picks = ((held[:, None] == jnp.arange(group * padded_count)) & my_live[:, None]).astype(bf16)
    group_teacher = jnp.dot(picks, group_teacher, preferred_element_type=f32).astype(bf16)
    group_teacher, every_student = lax.optimization_barrier((group_teacher, every_student))
    every_teacher = to_all(group_teacher, parts).reshape(-1, width)

    peak_s, lse_s, powers_s, terms_s = stored_powers(every_student, student_proto, student_temp, block, True)
    every_teacher, terms_s = lax.optimization_barrier((every_teacher, terms_s))
    peak_t, lse_t, powers_t = stored_powers(every_teacher, teacher_proto, teacher_temp, block, False)
    every_lse = to_all(jnp.concatenate([lse_t, lse_s])[None], parts)
    terms_t = row_terms(powers_t, student_proto, block)
    every_lse, terms_t = lax.optimization_barrier((every_lse, terms_t))
    top = jnp.max(every_lse, axis=0)
    lse = (top + jnp.log2(jnp.sum(jnp.exp2(every_lse - top), axis=0)))[0]
    rows_total = every_student.shape[0]
    scale_t = jnp.exp2(peak_t - lse[:rows_total] + log_weight)
    scale_s = jnp.exp2(peak_s - lse[rows_total:] + log_weight)
    my_terms = combined_terms(scale_s, scale_t, terms_s, terms_t, block)
    terms = lax.all_to_all(my_terms.reshape(parts, capacity, width), "dp", 0, 0)
    grad_proto = proto_gradient(every_student, scale_s, scale_t, powers_s, powers_t, block)
    terms, grad_proto = lax.optimization_barrier((terms, grad_proto))
    feature_grad = jnp.sum(terms.astype(f32), axis=0)
    along_unit = jnp.sum(student_float * feature_grad, axis=-1, keepdims=True)
    unit_grad = ((feature_grad - student_float * along_unit) / lengths).astype(bf16)
    partial_bottleneck = lax.dot_general(
        student_rows, unit_grad, (((0,), (0,)), ((), ())), preferred_element_type=f32
    ).astype(bf16)
    pieces = lax.all_to_all(partial_bottleneck.reshape(parts, -1, width), "dp", 0, 0)
    grad_bottleneck = jnp.sum(pieces.astype(f32), axis=0)
    spread_grad = lax.dot_general(
        spread, unit_grad, (((0,), (0,)), ((), ())), preferred_element_type=f32
    ).astype(bf16)
    grad_rows = lax.dot_general(
        spread_grad, student_bottleneck, (((1,), (1,)), ((), ())), preferred_element_type=f32
    ).astype(bf16)
    return grad_proto, grad_bottleneck, grad_rows.reshape(images, slot_count, grad_rows.shape[-1])


def on_device(
    teacher_feat,
    teacher_bottleneck,
    teacher_proto,
    student_feat,
    student_bottleneck,
    student_proto,
    mask_index,
    mask_count,
    *,
    parts,
    group,
):
    images, masked = mask_index.shape
    full = images * (masked + 1)
    capacities = [c for c in (104, 112) if c < full] + [full]
    needed = jnp.max(jnp.sum(mask_count.reshape(parts, images) + 1, axis=-1))
    branch = sum((needed > c).astype(jnp.int32) for c in capacities[:-1])
    outs = lax.switch(
        branch,
        [functools.partial(packed_step, parts=parts, group=group, capacity=c) for c in capacities],
        teacher_feat,
        teacher_bottleneck,
        teacher_proto,
        student_feat[0],
        student_bottleneck[0],
        student_proto[0],
        mask_index,
        mask_count,
    )
    return tuple(out[None] for out in outs)


def solution(mesh):
    in_specs = (
        P(("dp", "group"), None, None),
        P(),
        P(None, "dp"),
        P("group", "dp", None, None),
        P("group", None, None),
        P("group", None, "dp"),
        P("dp", None),
        P(),
    )
    out_specs = (P("group", None, "dp"), P("group", "dp", None), P("group", "dp", None, None))
    step = functools.partial(on_device, parts=mesh.shape["dp"], group=mesh.shape["group"])
    return jax.shard_map(step, mesh=mesh, in_specs=in_specs, out_specs=out_specs, check_vma=False)
```

profile of v0, /device:TPU:0, one launch (start us, length us, event | category | flops | bytes accessed | tf_op | source)
XLA Modules:
  0.0 173.4 jit_solution(14427074157120428761)
XLA Ops:
  3.5 169.2 %conditional.1 = (f32[256,2048]{1,0:T(8,128)}, f32[1,32,256]{2,1,0:T(8,128)S(1)}, bf16[1,8,17,1024]{3,1,2,0:T(8,128)(2,1)S(1)}) conditional(s32[]{:T(128)} %clamp.3, (s32[256]{0:T(256)}, s32[8,16]{1,0:T(8,128)}, bf16[2,257,4096]{2,0,1:T(2,128)(2,1)}, bf16[4096,256]{1,0:T(8,128)(2,1)}, bf16[8,257,1024]{2,0,1:T(8,128)(2,1)}, ...), branch_computations={%region_2.16_spmd, %region_16.30_spmd, %region_30.44_spmd} | conditional | flops 23134525440 | bytes 196707808 | solution.py:276
  4.8 0.8 concatenate.30
  5.8 4.4 %gather_fusion.1 = bf16[104,1024]{1,0:T(8,128)(2,1)S(1)} fusion(bf16[8,257,1024]{2,0,1:T(8,128)(2,1)} %get-tuple-element.54, s32[104]{0:T(128)S(1)} %fusion.36), kind=kCustom, calls=%fused_computation.1 | custom fusion | bytes 426816 | tf_op jit(solution)/shard_map/cond/branch_0_fun/gather | solution.py:207
  11.3 1.3 broadcast_in_dim.198
  12.6 10.7 %all-to-all-start = ((bf16[32,104,256]{2,1,0:T(8,128)(2,1)}), bf16[32,104,256]{2,1,0:T(8,128)(2,1)S(1)}, u32[]{:S(2)}, u32[]{:S(2)}) async-start(bf16[32,104,256]{2,1,0:T(8,128)(2,1)} %broadcast_in_dim.198), calls=%async_computation | async-start | bytes 3407872 | tf_op jit(solution)/shard_map/cond/branch_0_fun/all_to_all | solution.py:159
  23.5 2.4 %gather_fusion = bf16[34,4096]{1,0:T(8,128)(2,1)S(1)} fusion(bf16[2,257,4096]{2,0,1:T(2,128)(2,1)} %get-tuple-element.51, s32[34]{0:T(128)S(1)} %reshape.825), kind=kCustom, calls=%fused_computation | custom fusion | bytes 557328 | tf_op jit(solution)/shard_map/cond/branch_0_fun/gather | solution.py:214
  25.9 2.1 %multiply_reduce_fusion.2 = (f32[34]{0:T(128)S(1)}, f32[34,256]{1,0:T(8,128)S(1)}) fusion(bf16[34,4096]{1,0:T(8,128)(2,1)S(1)} %gather_fusion, bf16[4096,256]{1,0:T(8,128)(2,1)} %get-tuple-element.53), kind=kOutput, calls=%fused_computation.41 | convolution fusion | flops 71320544 | bytes 2410632 | tf_op jit(solution)/shard_map/cond/branch_0_fun/dot_general | solution.py:215
  28.4 1.0 collective-permute-start.1
  30.1 11.0 %collective-permute-done.2 = bf16[48,256]{1,0:T(8,128)(2,1)S(1)} collective-permute-done((bf16[48,256]{1,0:T(8,128)(2,1)S(1)}, bf16[48,256]{1,0:T(8,128)(2,1)S(1)}, u32[]{:S(2)}, u32[]{:S(2)}) %collective-permute-start.2) | collective-permute-done | bytes 24608 | tf_op jit(solution)/shard_map/cond/branch_0_fun/ppermute | solution.py:217
  41.0 1.8 %collective-permute-done.1 = bf16[48,256]{1,0:T(8,128)(2,1)S(1)} collective-permute-done((bf16[48,256]{1,0:T(8,128)(2,1)S(1)}, bf16[48,256]{1,0:T(8,128)(2,1)S(1)}, u32[]{:S(2)}, u32[]{:S(2)}) %collective-permute-start.1) | collective-permute-done | bytes 24608 | tf_op jit(solution)/shard_map/cond/branch_0_fun/ppermute | solution.py:217
  43.0 5.4 %all-to-all-done = bf16[32,104,256]{2,1,0:T(8,128)(2,1)S(1)} async-done(((bf16[32,104,256]{2,1,0:T(8,128)(2,1)}), bf16[32,104,256]{2,1,0:T(8,128)(2,1)S(1)}, u32[]{:S(2)}, u32[]{:S(2)}) %all-to-all-start) | async-done | bytes 1703968 | tf_op jit(solution)/shard_map/cond/branch_0_fun/all_to_all | solution.py:159
  48.4 1.3 broadcast_in_dim.199
  49.7 7.1 %all-to-all-start.1 = ((bf16[32,104,256]{2,1,0:T(8,128)(2,1)}), bf16[32,104,256]{2,1,0:T(8,128)(2,1)S(1)}, u32[]{:S(2)}, u32[]{:S(2)}) async-start(bf16[32,104,256]{2,1,0:T(8,128)(2,1)} %broadcast_in_dim.199), calls=%async_computation.1 | async-start | bytes 3407872 | tf_op jit(solution)/shard_map/cond/branch_0_fun/all_to_all | solution.py:159
  56.8 17.9 %branch_0_fun.5 = (f32[4,1,832]{2,1,0:T(1,128)S(1)}, f32[4,1,832]{2,1,0:T(1,128)S(1)}, bf16[3328,2048]{1,0:T(8,128)(2,1)}, bf16[3328,256]{1,0:T(8,128)(2,1)S(1)}) custom-call(bf16[3328,256]{1,0:T(8,128)(2,1)S(1)} %bitcast.138, bf16[256,2048]{1,0:T(8,128)(2,1)} %get-tuple-element.57.proto_ref), custom_call_target="tpu_custom_call" | custom-call | flops 6979321856 | bytes 13631488 | tf_op jit(solution)/shard_map/cond/branch_0_fun/pallas_call | solution.py:76
  74.8 1.2 copy-done.10
  76.1 6.1 %all-to-all-done.1 = bf16[32,104,256]{2,1,0:T(8,128)(2,1)S(1)} async-done(((bf16[32,104,256]{2,1,0:T(8,128)(2,1)}), bf16[32,104,256]{2,1,0:T(8,128)(2,1)S(1)}, u32[]{:S(2)}, u32[]{:S(2)}) %all-to-all-start.1) | async-done | bytes 1703968 | tf_op jit(solution)/shard_map/cond/branch_0_fun/all_to_all | solution.py:159
  82.1 12.2 %branch_0_fun.6 = (f32[4,1,832]{2,1,0:T(1,128)S(1)}, f32[4,1,832]{2,1,0:T(1,128)S(1)}, bf16[3328,2048]{1,0:T(8,128)(2,1)}) custom-call(bf16[3328,256]{1,0:T(8,128)(2,1)S(1)} %bitcast.140, bf16[256,2048]{1,0:T(8,128)(2,1)} %get-tuple-element.62.proto_ref), custom_call_target="tpu_custom_call" | custom-call | flops 3489660928 | bytes 13631488 | tf_op jit(solution)/shard_map/cond/branch_0_fun/pallas_call | solution.py:76
  94.5 1.3 broadcast_in_dim.200
  95.9 4.8 %all-to-all-start.2 = ((f32[32,1,6656]{2,1,0:T(1,128)}), f32[32,1,6656]{2,1,0:T(1,128)}, u32[]{:S(2)}, u32[]{:S(2)}) async-start(f32[32,1,6656]{2,1,0:T(1,128)} %broadcast_in_dim.200), calls=%async_computation.2 | async-start | bytes 1703936 | tf_op jit(solution)/shard_map/cond/branch_0_fun/all_to_all | solution.py:159
  101.1 7.7 %branch_0_fun.7.terms_t_ref = bf16[3328,256]{1,0:T(8,128)(2,1)S(1)} custom-call(bf16[3328,2048]{1,0:T(8,128)(2,1)} %get-tuple-element.65.powers_ref.powers_t_ref, bf16[256,2048]{1,0:T(8,128)(2,1)} %get-tuple-element.57.proto_ref), custom_call_target="tpu_custom_call" | custom-call | flops 3489660928 | bytes 13631488 | tf_op jit(solution)/shard_map/cond/branch_0_fun/pallas_call | solution.py:97
  108.8 7.5 %all-to-all-done.2 = f32[32,1,6656]{2,1,0:T(1,128)} async-done(((f32[32,1,6656]{2,1,0:T(1,128)}), f32[32,1,6656]{2,1,0:T(1,128)}, u32[]{:S(2)}, u32[]{:S(2)}) %all-to-all-start.2) | async-done | bytes 852000 | tf_op jit(solution)/shard_map/cond/branch_0_fun/all_to_all | solution.py:159
  116.4 1.6 reduce_max.32
  118.0 1.3 fusion.2
  119.7 1.4 copy-done.11
  121.2 3.2 %branch_0_fun.8 = bf16[3328,256]{1,0:T(8,128)(2,1)} custom-call(f32[4,1,832]{2,1,0:T(1,128)S(1)} %get-tuple-element.157.scale_s_ref, f32[4,1,832]{2,1,0:T(1,128)S(1)} %get-tuple-element.156.scale_t_ref, bf16[3328,256]{1,0:T(8,128)(2,1)S(1)} %copy-done.11, bf16[3328,256]{1,0:T(8,128)(2,1)S(1)} %branch_0_fun.7.terms_t_ref), custom_call_target="tpu_custom_call" | custom-call | flops 2555904 | bytes 5111808 | tf_op jit(solution)/shard_map/cond/branch_0_fun/pallas_call | solution.py:117
  124.4 4.6 %all-to-all-start.3 = ((bf16[32,104,256]{2,1,0:T(8,128)(2,1)}), bf16[32,104,256]{2,1,0:T(8,128)(2,1)S(1)}, u32[]{:S(2)}, u32[]{:S(2)}) async-start(bf16[32,104,256]{2,1,0:T(8,128)(2,1)} %bitcast.9), calls=%async_computation.3 | async-start | bytes 3407872 | tf_op jit(solution)/shard_map/cond/branch_0_fun/all_to_all | solution.py:238
  129.1 13.9 %branch_0_fun.9 = f32[256,2048]{1,0:T(8,128)} custom-call(bf16[3328,256]{1,0:T(8,128)(2,1)S(1)} %bitcast.139, f32[4,1,832]{2,1,0:T(1,128)S(1)} %get-tuple-element.157.scale_s_ref, f32[4,1,832]{2,1,0:T(1,128)S(1)} %get-tuple-element.156.scale_t_ref, bf16[3328,2048]{1,0:T(8,128)(2,1)} %get-tuple-element.70.powers_s_ref, ...), custom_call_target="tpu_custom_call" | custom-call | flops 3489660928 | bytes 27262976 | tf_op jit(solution)/shard_map/cond/branch_0_fun/pallas_call | solution.py:145
  143.0 9.7 %all-to-all-done.3 = bf16[32,104,256]{2,1,0:T(8,128)(2,1)S(1)} async-done(((bf16[32,104,256]{2,1,0:T(8,128)(2,1)}), bf16[32,104,256]{2,1,0:T(8,128)(2,1)S(1)}, u32[]{:S(2)}, u32[]{:S(2)}) %all-to-all-start.3) | async-done | bytes 1703968 | tf_op jit(solution)/shard_map/cond/branch_0_fun/all_to_all | solution.py:238
  152.9 1.1 multiply_reduce_fusion
  154.0 2.2 %convolution_convert_fusion = bf16[1024,256]{1,0:T(8,128)(2,1)} fusion(bf16[104,1024]{1,0:T(8,128)(2,1)} %copy-done.26, f32[104,256]{1,0:T(8,128)S(1)} %convert_reduce_fusion, f32[104]{0:T(128)S(1)} %multiply_reduce_fusion, f32[104]{0:T(128)S(1)} %add_sqrt_fusion, f32[104,256]{1,0:T(8,128)} %copy-done.22), kind=kOutput, calls=%fused_computation.7 | convolution fusion | flops 54921216 | bytes 951104 | tf_op jit(solution)/shard_map/cond/branch_0_fun/dot_general | solution.py:244
  156.2 4.5 %all-to-all-start.4 = ((bf16[32,32,256]{2,1,0:T(8,128)(2,1)}), bf16[32,32,256]{2,1,0:T(8,128)(2,1)S(1)}, u32[]{:S(2)}, u32[]{:S(2)}) async-start(bf16[32,32,256]{2,1,0:T(8,128)(2,1)} %bitcast.10), calls=%async_computation.4 | async-start | bytes 1048576 | tf_op jit(solution)/shard_map/cond/branch_0_fun/all_to_all | solution.py:247
  161.5 10.6 %all-to-all-done.4 = bf16[32,32,256]{2,1,0:T(8,128)(2,1)S(1)} async-done(((bf16[32,32,256]{2,1,0:T(8,128)(2,1)}), bf16[32,32,256]{2,1,0:T(8,128)(2,1)S(1)}, u32[]{:S(2)}, u32[]{:S(2)}) %all-to-all-start.4) | async-done | bytes 524320 | tf_op jit(solution)/shard_map/cond/branch_0_fun/all_to_all | solution.py:247
  (68 shorter events, 8.3 us)
Async XLA Ops:
  3.5 6.8 %copy-start.14 = (bf16[1024,256]{1,0:T(8,128)(2,1)S(1)}, bf16[1024,256]{1,0:T(8,128)(2,1)}, u32[]{:S(2)}) copy-start(bf16[1024,256]{1,0:T(8,128)(2,1)} %get-tuple-element.55) | copy-start | bytes 1572868 | tf_op jit(solution)/shard_map/cond
  10.2 2.4 %copy-start.26 = (bf16[104,1024]{1,0:T(8,128)(2,1)}, bf16[104,1024]{1,0:T(8,128)(2,1)S(1)}, u32[]{:S(2)}) copy-start(bf16[104,1024]{1,0:T(8,128)(2,1)S(1)} %gather_fusion.1) | copy-start | bytes 638980 | tf_op jit(solution)/shard_map/cond
  10.5 0.7 copy-start.22
  12.6 10.8 %copy-start.28 = (s32[8,16]{1,0:T(8,128)S(1)}, s32[8,16]{1,0:T(8,128)}, u32[]{:S(2)}) copy-start(s32[8,16]{1,0:T(8,128)} %get-tuple-element.52) | copy-start | bytes 1540 | tf_op jit(solution)/shard_map/cond
  12.6 35.8 %all-to-all-start = ((bf16[32,104,256]{2,1,0:T(8,128)(2,1)}), bf16[32,104,256]{2,1,0:T(8,128)(2,1)S(1)}, u32[]{:S(2)}, u32[]{:S(2)}) async-start(bf16[32,104,256]{2,1,0:T(8,128)(2,1)} %broadcast_in_dim.198), calls=%async_computation | async-start | bytes 3407872 | tf_op jit(solution)/shard_map/cond/branch_0_fun/all_to_all | solution.py:159
  28.1 12.9 %collective-permute-start.2 = (bf16[48,256]{1,0:T(8,128)(2,1)S(1)}, bf16[48,256]{1,0:T(8,128)(2,1)S(1)}, u32[]{:S(2)}, u32[]{:S(2)}) collective-permute-start(bf16[48,256]{1,0:T(8,128)(2,1)S(1)} %pad.10), channel_id=1, source_target_pairs={{0,96},{32,64},{64,32},{96,0},{1,97},{33,65},{65,33},{97,1},{2,98}... | collective-permute-start | bytes 73736 | tf_op jit(solution)/shard_map/cond/branch_0_fun/ppermute | solution.py:217
  28.4 14.4 %collective-permute-start.1 = (bf16[48,256]{1,0:T(8,128)(2,1)S(1)}, bf16[48,256]{1,0:T(8,128)(2,1)S(1)}, u32[]{:S(2)}, u32[]{:S(2)}) collective-permute-start(bf16[48,256]{1,0:T(8,128)(2,1)S(1)} %pad.10), channel_id=1, source_target_pairs={{0,64},{32,96},{64,0},{96,32},{1,65},{33,97},{65,1},{97,33},{2,66}... | collective-permute-start | bytes 73736 | tf_op jit(solution)/shard_map/cond/branch_0_fun/ppermute | solution.py:217
  29.4 13.4 %collective-permute-start = (bf16[48,256]{1,0:T(8,128)(2,1)S(1)}, bf16[48,256]{1,0:T(8,128)(2,1)S(1)}, u32[]{:S(2)}, u32[]{:S(2)}) collective-permute-start(bf16[48,256]{1,0:T(8,128)(2,1)S(1)} %pad.10), channel_id=1, source_target_pairs={{0,32},{32,0},{64,96},{96,64},{1,33},{33,1},{65,97},{97,65},{2,34}... | collective-permute-start | bytes 73736 | tf_op jit(solution)/shard_map/cond/branch_0_fun/ppermute | solution.py:217
  49.7 32.4 %all-to-all-start.1 = ((bf16[32,104,256]{2,1,0:T(8,128)(2,1)}), bf16[32,104,256]{2,1,0:T(8,128)(2,1)S(1)}, u32[]{:S(2)}, u32[]{:S(2)}) async-start(bf16[32,104,256]{2,1,0:T(8,128)(2,1)} %broadcast_in_dim.199), calls=%async_computation.1 | async-start | bytes 3407872 | tf_op jit(solution)/shard_map/cond/branch_0_fun/all_to_all | solution.py:159
  74.8 1.2 copy-start.10
  94.4 6.3 %copy-start.33 = (s32[256]{0:T(256)S(1)}, s32[256]{0:T(256)}, u32[]{:S(2)}) copy-start(s32[256]{0:T(256)} %get-tuple-element.50) | copy-start | bytes 3076 | tf_op jit(solution)/shard_map/cond
  95.9 20.5 %all-to-all-start.2 = ((f32[32,1,6656]{2,1,0:T(1,128)}), f32[32,1,6656]{2,1,0:T(1,128)}, u32[]{:S(2)}, u32[]{:S(2)}) async-start(f32[32,1,6656]{2,1,0:T(1,128)} %broadcast_in_dim.200), calls=%async_computation.2 | async-start | bytes 1703936 | tf_op jit(solution)/shard_map/cond/branch_0_fun/all_to_all | solution.py:159
  119.7 1.5 copy-start.11
  124.4 28.3 %all-to-all-start.3 = ((bf16[32,104,256]{2,1,0:T(8,128)(2,1)}), bf16[32,104,256]{2,1,0:T(8,128)(2,1)S(1)}, u32[]{:S(2)}, u32[]{:S(2)}) async-start(bf16[32,104,256]{2,1,0:T(8,128)(2,1)} %bitcast.9), calls=%async_computation.3 | async-start | bytes 3407872 | tf_op jit(solution)/shard_map/cond/branch_0_fun/all_to_all | solution.py:238
  143.0 17.7 %copy-start.15 = (bf16[1024,256]{1,0:T(8,128)(2,1)S(1)}, bf16[1024,256]{1,0:T(8,128)(2,1)}, u32[]{:S(2)}) copy-start(bf16[1024,256]{1,0:T(8,128)(2,1)} %get-tuple-element.55) | copy-start | bytes 1572868 | tf_op jit(solution)/shard_map/cond
  143.0 17.7 %copy-start.23 = (f32[104,256]{1,0:T(8,128)S(1)}, f32[104,256]{1,0:T(8,128)}, u32[]{:S(2)}) copy-start(f32[104,256]{1,0:T(8,128)} %copy-done.22) | copy-start | bytes 319492 | tf_op jit(solution)/shard_map/cond
  156.2 15.9 %all-to-all-start.4 = ((bf16[32,32,256]{2,1,0:T(8,128)(2,1)}), bf16[32,32,256]{2,1,0:T(8,128)(2,1)S(1)}, u32[]{:S(2)}, u32[]{:S(2)}) async-start(bf16[32,32,256]{2,1,0:T(8,128)(2,1)} %bitcast.10), calls=%async_computation.4 | async-start | bytes 1048576 | tf_op jit(solution)/shard_map/cond/branch_0_fun/all_to_all | solution.py:247
  172.6 0.7 copy-start.27
  172.7 0.7 copy-start.38
where the time goes:
time: 174 us; the launch traced here: 173 us
  Pallas kernels  55 us (32%)
  waiting for transfers between devices  52 us (30%)
  starting transfers between devices  33.7 us (19%)
  local copies, waits for them, and re-layouts  16.6 us (10%)
  other arithmetic  7.89 us (5%)
  matrix products  5.28 us (3%)
  between operations  1.96 us (1%)
    pallas_call x2, Pallas kernels, stored_powers(): pl.pallas_call(functools.partial(powers_terms_kernel if fused else powers...  30.2 us
    all_to_all x3, starting transfers between devices, to_all(): lax.all_to_all(jnp.broadcast_to(block[None], (parts,) + block.shape), 'dp...  22.6 us
    all_to_all x3, waiting for transfers between devices, to_all(): lax.all_to_all(jnp.broadcast_to(block[None], (parts,) + block.shape), 'dp...  19 us
    pallas_call x1, Pallas kernels, proto_gradient(): pl.pallas_call(functools.partial(grads_kernel, tile), grid=(steps,), in_s...  13.9 us
    ppermute x3, waiting for transfers between devices, packed_step(): lax.ppermute(teacher_unit, 'group', [(i, i ^ k) for i in range(group)])  12.8 us
    all_to_all x1, waiting for transfers between devices, packed_step(): lax.all_to_all(partial_bottleneck.reshape(parts, -1, width), 'dp', 0, 0)  10.6 us
    all_to_all x1, waiting for transfers between devices, packed_step(): terms = lax.all_to_all(my_terms.reshape(parts, capacity, width), 'dp', 0, 0)  9.7 us
    pallas_call x1, Pallas kernels, row_terms(): pl.pallas_call(terms_kernel, grid=(count // block,), in_specs=[row_block(...  7.72 us
  transfers between devices with their start and end apart: 8, of which 7 were waited for; matrix products, arithmetic and copies ran while one was open for 4% of the time, Pallas kernels for 23%

commit v1 on v0

--- a/solution.py
+++ b/solution.py
@@ -84,7 +84,7 @@
             flops=2 * (1 + fused) * count * proto.size, bytes_accessed=2 * count * columns, transcendentals=count * columns
         ),
     )(rows, proto)
-    return peak.reshape(count), lse.reshape(count), *stored
+    return peak, lse, *stored
 
 
 def terms_kernel(powers_ref, proto_ref, terms_ref):
@@ -105,24 +105,44 @@
     )(powers, proto)
 
 
-def combine_kernel(scale_s_ref, scale_t_ref, terms_s_ref, terms_t_ref, out_ref):
-    student = column_of(scale_s_ref[0]) * terms_s_ref[...].astype(f32)
-    teacher = column_of(scale_t_ref[0]) * terms_t_ref[...].astype(f32)
+def total_lse(parts_lse):
+    top = jnp.max(parts_lse, axis=0)
+    return top + jnp.log2(jnp.sum(jnp.exp2(parts_lse - top), axis=0))
+
+
+def combine_kernel(lse_s_ref, lse_t_ref, peak_s_ref, peak_t_ref, weight_ref, terms_s_ref, terms_t_ref,
+                   out_ref, scale_s_ref, scale_t_ref):
+    scale_s = jnp.exp2(peak_s_ref[0] - total_lse(lse_s_ref[:, 0]) + weight_ref[0])
+    scale_t = jnp.exp2(peak_t_ref[0] - total_lse(lse_t_ref[:, 0]) + weight_ref[0])
+    scale_s_ref[0] = scale_s
+    scale_t_ref[0] = scale_t
+    student = column_of(scale_s) * terms_s_ref[...].astype(f32)
+    teacher = column_of(scale_t) * terms_t_ref[...].astype(f32)
     out_ref[...] = (student - teacher).astype(bf16)
 
 
-def combined_terms(scale_s, scale_t, terms_s, terms_t, block):
+def combined_terms(every_lse, peak_s, peak_t, log_weight, terms_s, terms_t):
     count, width = terms_s.shape
-    steps = count // block
+    steps, _, block = peak_s.shape
+    parts = every_lse.shape[0]
+    lanes = jax.ShapeDtypeStruct(peak_s.shape, f32)
     return pl.pallas_call(
         combine_kernel,
         grid=(steps,),
-        in_specs=[lane_block(block), lane_block(block), row_block(block, width), row_block(block, width)],
-        out_specs=row_block(block, width),
-        out_shape=jax.ShapeDtypeStruct((count, width), bf16),
+        in_specs=[
+            pl.BlockSpec((parts, 1, 1, block), lambda i: (0, i, 0, 0)),
+            pl.BlockSpec((parts, 1, 1, block), lambda i: (0, i + steps, 0, 0)),
+            lane_block(block),
+            lane_block(block),
+            lane_block(block),
+            row_block(block, width),
+            row_block(block, width),
+        ],
+        out_specs=[row_block(block, width), lane_block(block), lane_block(block)],
+        out_shape=[jax.ShapeDtypeStruct((count, width), bf16), lanes, lanes],
         compiler_params=vmem(24),
-        cost_estimate=pl.CostEstimate(flops=3 * count * width, bytes_accessed=6 * count * width, transcendentals=0),
-    )(scale_s.reshape(steps, 1, block), scale_t.reshape(steps, 1, block), terms_s, terms_t)
+        cost_estimate=pl.CostEstimate(flops=3 * count * width, bytes_accessed=6 * count * width, transcendentals=64 * count),
+    )(every_lse, every_lse, peak_s, peak_t, log_weight, terms_s, terms_t)
 
 
 def grads_kernel(tile, student_ref, scale_s_ref, scale_t_ref, powers_s_ref, powers_t_ref, grad_ref):
@@ -152,7 +172,7 @@
         cost_estimate=pl.CostEstimate(
             flops=2 * count * width * columns, bytes_accessed=4 * count * columns, transcendentals=0
         ),
-    )(student, scale_s.reshape(steps, 1, block), scale_t.reshape(steps, 1, block), powers_s, powers_t)
+    )(student, scale_s, scale_t, powers_s, powers_t)
 
 
 def to_all(block, parts):
@@ -226,15 +246,12 @@
     peak_s, lse_s, powers_s, terms_s = stored_powers(every_student, student_proto, student_temp, block, True)
     every_teacher, terms_s = lax.optimization_barrier((every_teacher, terms_s))
     peak_t, lse_t, powers_t = stored_powers(every_teacher, teacher_proto, teacher_temp, block, False)
-    every_lse = to_all(jnp.concatenate([lse_t, lse_s])[None], parts)
+    every_lse = to_all(jnp.concatenate([lse_s, lse_t]), parts)
     terms_t = row_terms(powers_t, student_proto, block)
     every_lse, terms_t = lax.optimization_barrier((every_lse, terms_t))
-    top = jnp.max(every_lse, axis=0)
-    lse = (top + jnp.log2(jnp.sum(jnp.exp2(every_lse - top), axis=0)))[0]
-    rows_total = every_student.shape[0]
-    scale_t = jnp.exp2(peak_t - lse[:rows_total] + log_weight)
-    scale_s = jnp.exp2(peak_s - lse[rows_total:] + log_weight)
-    my_terms = combined_terms(scale_s, scale_t, terms_s, terms_t, block)
+    my_terms, scale_s, scale_t = combined_terms(
+        every_lse, peak_s, peak_t, log_weight.reshape(peak_s.shape), terms_s, terms_t
+    )
     terms = lax.all_to_all(my_terms.reshape(parts, capacity, width), "dp", 0, 0)
     grad_proto = proto_gradient(every_student, scale_s, scale_t, powers_s, powers_t, block)
     terms, grad_proto = lax.optimization_barrier((terms, grad_proto))

time: 174 us -> 182 us (1.046); the launches traced: 173 us -> 185 us
  Pallas kernels: 55 us -> 63.7 us
  loops' own time: 0.85 us -> 4.3 us
  other arithmetic: 7.89 us -> 5.36 us
    another operation x1, loops' own time: 0.85 us -> 4.3 us  [on_device(): lax.switch(branch, [functools.partial(packed_step, parts=parts, group=gro...]
    pallas_call x2, Pallas kernels: 30.2 us -> 33.4 us  [stored_powers(): pl.pallas_call(functools.partial(powers_terms_kernel if fused else powers...]
    pallas_call x1, Pallas kernels: 7.72 us -> 10.1 us  [row_terms(): pl.pallas_call(terms_kernel, grid=(count // block,), in_specs=[row_block(...]
    pallas_call x1, Pallas kernels: 13.9 us -> 16 us  [proto_gradient(): pl.pallas_call(functools.partial(grads_kernel, tile), grid=(steps,), in_s...]
    cond x19 -> x28, local copies, waits for them, and re-layouts: 3.46 us -> 5.55 us
  transfers between devices with their start and end apart: 8 -> 8, of which waited for: 7 -> 7; matrix products, arithmetic and copies ran while one was open for 4% -> 4% of each run, Pallas kernels for 23% -> 25%
where the time goes in v1:
time: 182 us; the launch traced here: 185 us
  Pallas kernels  63.7 us (35%)
  waiting for transfers between devices  51.3 us (28%)
  starting transfers between devices  35.3 us (19%)
  local copies, waits for them, and re-layouts  18.2 us (10%)
  other arithmetic  5.36 us (3%)
  loops' own time  4.3 us (2%)
  matrix products  4.26 us (2%)
  between operations  2.44 us (1%)
    pallas_call x2, Pallas kernels, stored_powers(): pl.pallas_call(functools.partial(powers_terms_kernel if fused else powers...  33.4 us
    all_to_all x3, starting transfers between devices, to_all(): lax.all_to_all(jnp.broadcast_to(block[None], (parts,) + block.shape), 'dp...  23.4 us
    all_to_all x3, waiting for transfers between devices, to_all(): lax.all_to_all(jnp.broadcast_to(block[None], (parts,) + block.shape), 'dp...  18.9 us
    pallas_call x1, Pallas kernels, proto_gradient(): pl.pallas_call(functools.partial(grads_kernel, tile), grid=(steps,), in_s...  16 us
    ppermute x3, waiting for transfers between devices, packed_step(): lax.ppermute(teacher_unit, 'group', [(i, i ^ k) for i in range(group)])  13.9 us
    pallas_call x1, Pallas kernels, row_terms(): pl.pallas_call(terms_kernel, grid=(count // block,), in_specs=[row_block(...  10.1 us
    all_to_all x1, waiting for transfers between devices, packed_step(): lax.all_to_all(partial_bottleneck.reshape(parts, -1, width), 'dp', 0, 0)  9.9 us
    all_to_all x1, waiting for transfers between devices, packed_step(): terms = lax.all_to_all(my_terms.reshape(parts, capacity, width), 'dp', 0, 0)  8.58 us
  transfers between devices with their start and end apart: 8, of which 7 were waited for; matrix products, arithmetic and copies ran while one was open for 4% of the time, Pallas kernels for 25%

profile of v1, /device:TPU:0, one launch (start us, length us, event | category | flops | bytes accessed | tf_op | source)
XLA Modules:
  0.0 184.9 jit_solution(1439906702124179333)
XLA Ops:
  3.5 180.3 %conditional.1 = (f32[256,2048]{1,0:T(8,128)}, f32[1,32,256]{2,1,0:T(8,128)S(1)}, bf16[1,8,17,1024]{3,1,2,0:T(8,128)(2,1)}) conditional(s32[]{:T(128)} %clamp.3, (s32[256]{0:T(256)}, s32[8,16]{1,0:T(8,128)}, bf16[2,257,4096]{2,0,1:T(2,128)(2,1)}, bf16[4096,256]{1,0:T(8,128)(2,1)}, bf16[8,257,1024]{2,0,1:T(8,128)(2,1)}, ...), branch_computations={%region_2.14_spmd, %region_14.26_spmd, %region_26.38_spmd} | conditional | flops 23133382656 | bytes 194869952 | solution.py:293
  3.7 0.7 broadcast_add_fusion.1
  5.1 0.8 concatenate.35
  6.1 3.6 %gather_fusion.3 = bf16[112,1024]{1,0:T(8,128)(2,1)S(1)} fusion(bf16[8,257,1024]{2,0,1:T(8,128)(2,1)} %get-tuple-element.80, s32[112]{0:T(128)S(1)} %fusion.70), kind=kCustom, calls=%fused_computation.3 | custom fusion | bytes 459648 | tf_op jit(solution)/shard_map/cond/branch_1_fun/gather | solution.py:227
  10.8 1.3 broadcast_in_dim.226
  12.1 11.4 %all-to-all-start.5 = ((bf16[32,112,256]{2,1,0:T(8,128)(2,1)}), bf16[32,112,256]{2,1,0:T(8,128)(2,1)S(1)}, u32[]{:S(2)}, u32[]{:S(2)}) async-start(bf16[32,112,256]{2,1,0:T(8,128)(2,1)} %broadcast_in_dim.226), calls=%async_computation.5 | async-start | bytes 3670016 | tf_op jit(solution)/shard_map/cond/branch_1_fun/all_to_all | solution.py:179
  23.7 2.4 %gather_fusion.2 = bf16[34,4096]{1,0:T(8,128)(2,1)S(1)} fusion(bf16[2,257,4096]{2,0,1:T(2,128)(2,1)} %get-tuple-element.77, s32[34]{0:T(128)S(1)} %reshape.681), kind=kCustom, calls=%fused_computation.2 | custom fusion | bytes 557328 | tf_op jit(solution)/shard_map/cond/branch_1_fun/gather | solution.py:234
  26.1 2.1 %multiply_reduce_fusion.5 = (f32[34]{0:T(128)S(1)}, f32[34,256]{1,0:T(8,128)S(1)}) fusion(bf16[34,4096]{1,0:T(8,128)(2,1)S(1)} %gather_fusion.2, bf16[4096,256]{1,0:T(8,128)(2,1)} %get-tuple-element.79), kind=kOutput, calls=%fused_computation.109 | convolution fusion | flops 71320544 | bytes 2410632 | tf_op jit(solution)/shard_map/cond/branch_1_fun/dot_general | solution.py:235
  28.6 1.0 collective-permute-start.4
  30.3 13.4 %collective-permute-done.5 = bf16[48,256]{1,0:T(8,128)(2,1)S(1)} collective-permute-done((bf16[48,256]{1,0:T(8,128)(2,1)S(1)}, bf16[48,256]{1,0:T(8,128)(2,1)S(1)}, u32[]{:S(2)}, u32[]{:S(2)}) %collective-permute-start.5) | collective-permute-done | bytes 24608 | tf_op jit(solution)/shard_map/cond/branch_1_fun/ppermute | solution.py:237
  44.4 5.6 %all-to-all-done.5 = bf16[32,112,256]{2,1,0:T(8,128)(2,1)S(1)} async-done(((bf16[32,112,256]{2,1,0:T(8,128)(2,1)}), bf16[32,112,256]{2,1,0:T(8,128)(2,1)S(1)}, u32[]{:S(2)}, u32[]{:S(2)}) %all-to-all-start.5) | async-done | bytes 1835040 | tf_op jit(solution)/shard_map/cond/branch_1_fun/all_to_all | solution.py:179
  50.1 1.4 broadcast_in_dim.227
  51.5 7.2 %all-to-all-start.6 = ((bf16[32,112,256]{2,1,0:T(8,128)(2,1)}), bf16[32,112,256]{2,1,0:T(8,128)(2,1)}, u32[]{:S(2)}, u32[]{:S(2)}) async-start(bf16[32,112,256]{2,1,0:T(8,128)(2,1)} %broadcast_in_dim.227), calls=%async_computation.6 | async-start | bytes 3670016 | tf_op jit(solution)/shard_map/cond/branch_1_fun/all_to_all | solution.py:179
  58.7 19.5 %branch_1_fun.5 = (f32[8,1,448]{2,1,0:T(1,128)S(1)}, f32[8,1,448]{2,1,0:T(1,128)S(1)}, bf16[3584,2048]{1,0:T(8,128)(2,1)}, bf16[3584,256]{1,0:T(8,128)(2,1)S(1)}) custom-call(bf16[3584,256]{1,0:T(8,128)(2,1)S(1)} %bitcast.140, bf16[256,2048]{1,0:T(8,128)(2,1)S(1)} %copy-done.15), custom_call_target="tpu_custom_call" | custom-call | flops 7516192768 | bytes 14680064 | tf_op jit(solution)/shard_map/cond/branch_1_fun/pallas_call | solution.py:76
  78.3 1.3 copy-done.10
  79.5 6.0 %all-to-all-done.6 = bf16[32,112,256]{2,1,0:T(8,128)(2,1)} async-done(((bf16[32,112,256]{2,1,0:T(8,128)(2,1)}), bf16[32,112,256]{2,1,0:T(8,128)(2,1)}, u32[]{:S(2)}, u32[]{:S(2)}) %all-to-all-start.6) | async-done | bytes 1835040 | tf_op jit(solution)/shard_map/cond/branch_1_fun/all_to_all | solution.py:179
  85.6 13.8 %branch_1_fun.6 = (f32[8,1,448]{2,1,0:T(1,128)S(1)}, f32[8,1,448]{2,1,0:T(1,128)S(1)}, bf16[3584,2048]{1,0:T(8,128)(2,1)}) custom-call(bf16[3584,256]{1,0:T(8,128)(2,1)} %bitcast.20.rows_ref, bf16[256,2048]{1,0:T(8,128)(2,1)} %get-tuple-element.88.proto_ref), custom_call_target="tpu_custom_call" | custom-call | flops 3758096384 | bytes 14680064 | tf_op jit(solution)/shard_map/cond/branch_1_fun/pallas_call | solution.py:76
  99.4 1.9 %broadcast_in_dim.229 = f32[32,16,1,448]{3,2,1,0:T(1,128)} broadcast(f32[16,448]{1,0:T(8,128)S(1)} %bitcast.159), dimensions={1,3} | broadcast | bytes 946176 | tf_op jit(solution)/shard_map/cond/branch_1_fun/broadcast_in_dim | solution.py:179
  101.3 4.8 %all-to-all-start.7 = ((f32[32,16,1,448]{3,2,1,0:T(1,128)}), f32[32,16,1,448]{3,2,1,0:T(1,128)S(1)}, u32[]{:S(2)}, u32[]{:S(2)}) async-start(f32[32,16,1,448]{3,2,1,0:T(1,128)} %broadcast_in_dim.229), calls=%async_computation.7 | async-start | bytes 2097152 | tf_op jit(solution)/shard_map/cond/branch_1_fun/all_to_all | solution.py:179
  106.5 10.1 %branch_1_fun.7.terms_t_ref = bf16[3584,256]{1,0:T(8,128)(2,1)S(1)} custom-call(bf16[3584,2048]{1,0:T(8,128)(2,1)} %get-tuple-element.90.powers_ref.powers_t_ref, bf16[256,2048]{1,0:T(8,128)(2,1)} %get-tuple-element.83.proto_ref), custom_call_target="tpu_custom_call" | custom-call | flops 3758096384 | bytes 14680064 | tf_op jit(solution)/shard_map/cond/branch_1_fun/pallas_call | solution.py:97
  116.7 7.2 %all-to-all-done.7.lse_s_ref.lse_t_ref = f32[32,16,1,448]{3,2,1,0:T(1,128)S(1)} async-done(((f32[32,16,1,448]{3,2,1,0:T(1,128)}), f32[32,16,1,448]{3,2,1,0:T(1,128)S(1)}, u32[]{:S(2)}, u32[]{:S(2)}) %all-to-all-start.7) | async-done | bytes 917536 | tf_op jit(solution)/shard_map/cond/branch_1_fun/all_to_all | solution.py:179
  123.9 1.5 copy-done.11
  125.4 4.2 %branch_1_fun.8 = (bf16[3584,256]{1,0:T(8,128)(2,1)S(1)}, f32[8,1,448]{2,1,0:T(1,128)S(1)}, f32[8,1,448]{2,1,0:T(1,128)S(1)}) custom-call(f32[32,16,1,448]{3,2,1,0:T(1,128)S(1)} %all-to-all-done.7.lse_s_ref.lse_t_ref, f32[32,16,1,448]{3,2,1,0:T(1,128)S(1)} %all-to-all-done.7.lse_s_ref.lse_t_ref, f32[8,1,448]{2,1,0:T(1,128)S(1)} %get-tuple-element.92.peak_s_ref, ...), custom_call_target="tpu_custom_call" | custom-call | flops 2752512 | bytes 5505024 | tf_op jit(solution)/shard_map/cond/branch_1_fun/pallas_call | solution.py:129
  129.6 1.2 copy-done.9
  130.9 5.4 %all-to-all-start.8 = ((bf16[32,112,256]{2,1,0:T(8,128)(2,1)}), bf16[32,112,256]{2,1,0:T(8,128)(2,1)}, u32[]{:S(2)}, u32[]{:S(2)}) async-start(bf16[32,112,256]{2,1,0:T(8,128)(2,1)} %bitcast.145), calls=%async_computation.8 | async-start | bytes 3670016 | tf_op jit(solution)/shard_map/cond/branch_1_fun/all_to_all | solution.py:255
  136.3 16.0 %branch_1_fun.9 = f32[256,2048]{1,0:T(8,128)} custom-call(bf16[3584,256]{1,0:T(8,128)(2,1)S(1)} %bitcast.141, f32[8,1,448]{2,1,0:T(1,128)S(1)} %get-tuple-element.97.scale_s_ref, f32[8,1,448]{2,1,0:T(1,128)S(1)} %get-tuple-element.98.scale_t_ref, bf16[3584,2048]{1,0:T(8,128)(2,1)} %get-tuple-element.99.powers_s_ref, ...), custom_call_target="tpu_custom_call" | custom-call | flops 3758096384 | bytes 29360128 | tf_op jit(solution)/shard_map/cond/branch_1_fun/pallas_call | solution.py:165
  152.3 8.6 %all-to-all-done.8 = bf16[32,112,256]{2,1,0:T(8,128)(2,1)} async-done(((bf16[32,112,256]{2,1,0:T(8,128)(2,1)}), bf16[32,112,256]{2,1,0:T(8,128)(2,1)}, u32[]{:S(2)}, u32[]{:S(2)}) %all-to-all-start.8) | async-done | bytes 1835040 | tf_op jit(solution)/shard_map/cond/branch_1_fun/all_to_all | solution.py:255
  160.9 1.8 convert_reduce_fusion.2
  162.8 1.2 convolution_convert_fusion.4
  164.0 4.6 %all-to-all-start.9 = ((bf16[32,32,256]{2,1,0:T(8,128)(2,1)}), bf16[32,32,256]{2,1,0:T(8,128)(2,1)S(1)}, u32[]{:S(2)}, u32[]{:S(2)}) async-start(bf16[32,32,256]{2,1,0:T(8,128)(2,1)} %bitcast.22), calls=%async_computation.9 | async-start | bytes 1048576 | tf_op jit(solution)/shard_map/cond/branch_1_fun/all_to_all | solution.py:264
  169.2 0.9 copy.15
  170.1 9.9 %all-to-all-done.9 = bf16[32,32,256]{2,1,0:T(8,128)(2,1)S(1)} async-done(((bf16[32,32,256]{2,1,0:T(8,128)(2,1)}), bf16[32,32,256]{2,1,0:T(8,128)(2,1)S(1)}, u32[]{:S(2)}, u32[]{:S(2)}) %all-to-all-start.9) | async-done | bytes 524320 | tf_op jit(solution)/shard_map/cond/branch_1_fun/all_to_all | solution.py:264
  (63 shorter events, 7.2 us)
Async XLA Ops:
  3.7 6.0 %copy-start.19 = (bf16[1024,256]{1,0:T(8,128)(2,1)S(1)}, bf16[1024,256]{1,0:T(8,128)(2,1)}, u32[]{:S(2)}) copy-start(bf16[1024,256]{1,0:T(8,128)(2,1)} %get-tuple-element.81) | copy-start | bytes 1572868 | tf_op jit(solution)/shard_map/cond
  9.7 2.4 %copy-start.30 = (bf16[112,1024]{1,0:T(8,128)(2,1)}, bf16[112,1024]{1,0:T(8,128)(2,1)S(1)}, u32[]{:S(2)}) copy-start(bf16[112,1024]{1,0:T(8,128)(2,1)S(1)} %gather_fusion.3) | copy-start | bytes 688132 | tf_op jit(solution)/shard_map/cond
  10.0 0.6 copy-start.26
  12.1 11.5 %copy-start.35 = (s32[8,16]{1,0:T(8,128)S(1)}, s32[8,16]{1,0:T(8,128)}, u32[]{:S(2)}) copy-start(s32[8,16]{1,0:T(8,128)} %get-tuple-element.78) | copy-start | bytes 1540 | tf_op jit(solution)/shard_map/cond
  12.1 37.9 %all-to-all-start.5 = ((bf16[32,112,256]{2,1,0:T(8,128)(2,1)}), bf16[32,112,256]{2,1,0:T(8,128)(2,1)S(1)}, u32[]{:S(2)}, u32[]{:S(2)}) async-start(bf16[32,112,256]{2,1,0:T(8,128)(2,1)} %broadcast_in_dim.226), calls=%async_computation.5 | async-start | bytes 3670016 | tf_op jit(solution)/shard_map/cond/branch_1_fun/all_to_all | solution.py:179
  28.3 15.3 %collective-permute-start.5 = (bf16[48,256]{1,0:T(8,128)(2,1)S(1)}, bf16[48,256]{1,0:T(8,128)(2,1)S(1)}, u32[]{:S(2)}, u32[]{:S(2)}) collective-permute-start(bf16[48,256]{1,0:T(8,128)(2,1)S(1)} %pad.11), channel_id=1, source_target_pairs={{0,96},{32,64},{64,32},{96,0},{1,97},{33,65},{65,33},{97,1},{2,98}... | collective-permute-start | bytes 73736 | tf_op jit(solution)/shard_map/cond/branch_1_fun/ppermute | solution.py:237
  28.6 15.6 %collective-permute-start.4 = (bf16[48,256]{1,0:T(8,128)(2,1)S(1)}, bf16[48,256]{1,0:T(8,128)(2,1)S(1)}, u32[]{:S(2)}, u32[]{:S(2)}) collective-permute-start(bf16[48,256]{1,0:T(8,128)(2,1)S(1)} %pad.11), channel_id=1, source_target_pairs={{0,64},{32,96},{64,0},{96,32},{1,65},{33,97},{65,1},{97,33},{2,66}... | collective-permute-start | bytes 73736 | tf_op jit(solution)/shard_map/cond/branch_1_fun/ppermute | solution.py:237
  29.6 14.6 %collective-permute-start.3 = (bf16[48,256]{1,0:T(8,128)(2,1)S(1)}, bf16[48,256]{1,0:T(8,128)(2,1)S(1)}, u32[]{:S(2)}, u32[]{:S(2)}) collective-permute-start(bf16[48,256]{1,0:T(8,128)(2,1)S(1)} %pad.11), channel_id=1, source_target_pairs={{0,32},{32,0},{64,96},{96,64},{1,33},{33,1},{65,97},{97,65},{2,34}... | collective-permute-start | bytes 73736 | tf_op jit(solution)/shard_map/cond/branch_1_fun/ppermute | solution.py:237
  50.1 8.7 %copy-start.2 = (bf16[32,112,256]{2,1,0:T(8,128)(2,1)}, bf16[32,112,256]{2,1,0:T(8,128)(2,1)S(1)}, u32[]{:S(2)}) copy-start(bf16[32,112,256]{2,1,0:T(8,128)(2,1)S(1)} %all-to-all-done.5) | copy-start | bytes 5505028 | tf_op jit(solution)/shard_map/cond
  51.5 7.2 %copy-start.15 = (bf16[256,2048]{1,0:T(8,128)(2,1)S(1)}, bf16[256,2048]{1,0:T(8,128)(2,1)}, u32[]{:S(2)}) copy-start(bf16[256,2048]{1,0:T(8,128)(2,1)} %get-tuple-element.83.proto_ref) | copy-start | bytes 3145732 | tf_op jit(solution)/shard_map/cond
  51.5 34.0 %all-to-all-start.6 = ((bf16[32,112,256]{2,1,0:T(8,128)(2,1)}), bf16[32,112,256]{2,1,0:T(8,128)(2,1)}, u32[]{:S(2)}, u32[]{:S(2)}) async-start(bf16[32,112,256]{2,1,0:T(8,128)(2,1)} %broadcast_in_dim.227), calls=%async_computation.6 | async-start | bytes 3670016 | tf_op jit(solution)/shard_map/cond/branch_1_fun/all_to_all | solution.py:179
  78.3 1.3 copy-start.10
  99.4 6.7 %copy-start.38 = (s32[256]{0:T(256)S(1)}, s32[256]{0:T(256)}, u32[]{:S(2)}) copy-start(s32[256]{0:T(256)} %get-tuple-element.76) | copy-start | bytes 3076 | tf_op jit(solution)/shard_map/cond
  101.3 22.5 %all-to-all-start.7 = ((f32[32,16,1,448]{3,2,1,0:T(1,128)}), f32[32,16,1,448]{3,2,1,0:T(1,128)S(1)}, u32[]{:S(2)}, u32[]{:S(2)}) async-start(f32[32,16,1,448]{3,2,1,0:T(1,128)} %broadcast_in_dim.229), calls=%async_computation.7 | async-start | bytes 2097152 | tf_op jit(solution)/shard_map/cond/branch_1_fun/all_to_all | solution.py:179
  123.9 1.5 copy-start.11
  129.6 1.3 copy-start.9
  130.9 5.4 %copy-start.3 = (bf16[32,112,256]{2,1,0:T(8,128)(2,1)S(1)}, bf16[32,112,256]{2,1,0:T(8,128)(2,1)}, u32[]{:S(2)}) copy-start(bf16[32,112,256]{2,1,0:T(8,128)(2,1)} %copy-done.2) | copy-start | bytes 5505028 | tf_op jit(solution)/shard_map/cond
  130.9 30.0 %all-to-all-start.8 = ((bf16[32,112,256]{2,1,0:T(8,128)(2,1)}), bf16[32,112,256]{2,1,0:T(8,128)(2,1)}, u32[]{:S(2)}, u32[]{:S(2)}) async-start(bf16[32,112,256]{2,1,0:T(8,128)(2,1)} %bitcast.145), calls=%async_computation.8 | async-start | bytes 3670016 | tf_op jit(solution)/shard_map/cond/branch_1_fun/all_to_all | solution.py:255
  136.3 26.4 %copy-start.27 = (f32[112,256]{1,0:T(8,128)S(1)}, f32[112,256]{1,0:T(8,128)}, u32[]{:S(2)}) copy-start(f32[112,256]{1,0:T(8,128)} %copy-done.26) | copy-start | bytes 344068 | tf_op jit(solution)/shard_map/cond
  152.3 10.5 %copy-start.31 = (bf16[112,1024]{1,0:T(8,128)(2,1)S(1)}, bf16[112,1024]{1,0:T(8,128)(2,1)}, u32[]{:S(2)}) copy-start(bf16[112,1024]{1,0:T(8,128)(2,1)} %copy-done.30) | copy-start | bytes 688132 | tf_op jit(solution)/shard_map/cond
  164.0 16.0 %all-to-all-start.9 = ((bf16[32,32,256]{2,1,0:T(8,128)(2,1)}), bf16[32,32,256]{2,1,0:T(8,128)(2,1)S(1)}, u32[]{:S(2)}, u32[]{:S(2)}) async-start(bf16[32,32,256]{2,1,0:T(8,128)(2,1)} %bitcast.22), calls=%async_computation.9 | async-start | bytes 1048576 | tf_op jit(solution)/shard_map/cond/branch_1_fun/all_to_all | solution.py:264
  183.8 0.6 copy-start.40
